TPU v7x, 32 devices: a whole 2x2x4 slice. The times are simulated.
32 devices in a mesh: freq: 2 (over y), dom: 16 (over z, x, core).
Axes of the slice: x: 2, y: 2, z: 4, core: 2. Of those that a mesh axis runs over, the one named last changes fastest.
Arguments:
- fwd_source: float32 [4, 4, 512, 128], P('freq', None, 'dom'), may hold values from -6 to 6
- adj_source: float32 [4, 4, 512, 128], P('freq', None, 'dom'), may hold values from -6 to 6
- curl_blocks: float32 [512, 4, 128, 128], P('dom')
- block_links: int32 [512, 4], P('dom'), may hold values from 0 to 95, as said below
- tile_lists: int32 [64, 16], P('dom'), may hold values from 0 to 31, as said below
- edge_mass: float32 [512, 128], P('dom'), may hold values from 0.5 to 1.5
- omega: float32 [4], P('freq'), may hold values from 0.1 to 1
- cell_edges: int32 [12, 16384], P(None, 'dom'), may hold values from 0 to 4095
- log_cond: float32 [16384], P('dom'), may hold values from -6 to 6
Outputs:
- fwd_field: float32 [4, 4, 512, 128], P('freq', None, 'dom')
- adj_field: float32 [4, 4, 512, 128], P('freq', None, 'dom')
- model_next: float32 [16384], P('dom')
Inputs may be any that keep to these rules, and one draw needn't show every extreme that they name: `block_links`: entry 0 of each block row is the row's own local block; the others index the partition's extended field, local blocks first, then the tiles received in round 0, 1 and so on; every received tile is referenced by some row of the partition. `tile_lists`: the 16 blocks of one row are distinct local blocks.
All inputs are finite; a program needn't handle non-finite values.
Results may differ from a plain program's by a relative error of at most 0.0001.
Values sent between devices are 32-bit elements; how exact they have to be, the bound alone decides.
A program may use at most 64 MiB of HBM per device.

v0:
```python
import jax
import jax.numpy as jnp
from jax import lax
from jax.sharding import PartitionSpec as P

ITERS = 3


def swapped(value, axis, distance):
    mask = 2**distance
    pairs = [(source, source ^ mask) for source in range(lax.axis_size(axis))]
    return lax.ppermute(value, axis, pairs)


def operate(field, curl_blocks, block_links, tile_lists, weight, trade):
    parts = [field]
    for bit in range(tile_lists.shape[0]):
        outgoing = jnp.take(field, tile_lists[bit], axis=0)
        parts.append(trade(outgoing, bit))
    extended = jnp.concatenate(parts, axis=0)
    shape = field.shape
    gathered = jnp.take(extended, block_links.reshape(-1), axis=0)
    gathered = gathered.reshape(block_links.shape + shape[1:])
    curl = jnp.einsum("blij,blmj->bmi", curl_blocks, gathered, precision=lax.Precision.HIGHEST)
    count = weight.shape[2]
    curl = curl.reshape(shape[0], -1, count, 2, 2, shape[2])
    split = field.reshape(shape[0], -1, count, 2, 2, shape[2])
    real_part = curl[:, :, :, :, 0] - weight * split[:, :, :, :, 1]
    imag_part = curl[:, :, :, :, 1] + weight * split[:, :, :, :, 0]
    return jnp.stack([real_part, imag_part], axis=4).reshape(shape)


def chebyshev(source, curl_blocks, block_links, tile_lists, weight, trade):
    theta = 1.0
    delta = 0.7
    sone = theta / delta
    rho = 1.0 / sone
    solution = jnp.zeros_like(source)
    resid = source
    direction = source / theta
    for step in range(ITERS):
        solution = solution + direction
        if step + 1 < ITERS:
            resid = resid - operate(direction, curl_blocks, block_links, tile_lists, weight, trade)
            rho_new = 1.0 / (2.0 * sone - rho)
            direction = rho_new * rho * direction + 2.0 * rho_new / delta * resid
            rho = rho_new
    return solution


def to_rows(fields):
    shape = fields.shape
    moved = jnp.transpose(fields, (3, 0, 1, 2, 4))
    return moved.reshape(shape[3], shape[0] * shape[1] * shape[2], shape[4])


def from_rows(rows, systems, count):
    shaped = rows.reshape(rows.shape[0], systems, count, 4, rows.shape[2])
    return jnp.transpose(shaped, (1, 2, 3, 0, 4))


def local(
    fwd_source,
    adj_source,
    curl_blocks,
    block_links,
    tile_lists,
    edge_mass,
    omega,
    cell_edges,
    log_cond,
):
    count = fwd_source.shape[0]
    weight = (edge_mass[:, None, :] * omega[None, :, None])[:, None, :, None, :]

    def trade_one(outgoing, bit):
        return swapped(outgoing, "dom", bit)

    fwd_rows = chebyshev(
        to_rows(fwd_source[None]), curl_blocks, block_links, tile_lists, weight, trade_one
    )
    adj_rows = chebyshev(
        to_rows(adj_source[None]), curl_blocks, block_links, tile_lists, weight, trade_one
    )
    efield = from_rows(fwd_rows, 1, count)[0]
    lfield = from_rows(adj_rows, 1, count)[0]
    edges = efield.shape[2] * efield.shape[3]
    esplit = efield.reshape(count, 2, 2, edges)
    lsplit = lfield.reshape(count, 2, 2, edges)
    prod = esplit[:, :, 0] * lsplit[:, :, 1] + esplit[:, :, 1] * lsplit[:, :, 0]
    edge_term = jnp.sum(omega[:, None, None] * prod, axis=(0, 1))
    picked = jnp.take(edge_term, cell_edges.reshape(-1), axis=0).reshape(cell_edges.shape)
    scale = 1.0 / jnp.sqrt(24.0 * count * lax.axis_size("freq"))
    partial_grad = jnp.sum(picked, axis=0) * scale
    grad = lax.psum(partial_grad, "freq")
    model_next = log_cond - 0.5 * grad / jnp.sqrt(grad * grad + 1.0)
    return (efield, lfield, model_next)


def solution(mesh):
    in_specs = (
        P("freq", None, "dom", None),
        P("freq", None, "dom", None),
        P("dom", None, None, None),
        P("dom", None),
        P("dom", None),
        P("dom", None),
        P("freq"),
        P(None, "dom"),
        P("dom"),
    )
    out_specs = (P("freq", None, "dom", None), P("freq", None, "dom", None), P("dom"))
    return jax.shard_map(local, mesh=mesh, in_specs=in_specs, out_specs=out_specs, check_vma=False)
```

profile of v0, /device:TPU:0, one launch (start us, length us, event | category | flops | bytes accessed | tf_op | source)
XLA Modules:
  0.0 158.2 jit_solution(6203661800050647855)
XLA Ops:
  0.6 0.8 compare_and_fusion.1
  1.5 1.0 copy.47
  2.5 1.0 copy.51
  6.5 2.6 %collective-permute-start.1 = (f32[16,8,128]{2,1,0:T(8,128)S(1)}, f32[16,8,128]{2,1,0:T(8,128)S(1)}, u32[]{:S(2)}, u32[]{:S(2)}) collective-permute-start(f32[16,8,128]{2,1,0:T(8,128)S(1)} %get-tuple-element.60), channel_id=1, source_target_pairs={{0,2},{1,3},{2,0},{3,1},{4,6},{5,7},{6,4},{7,5},{8,10},{9,11},{10,... | collective-permute-start | bytes 196616 | tf_op jit(solution)/shard_map/ppermute | solution.py:12
  10.3 1.6 %collective-permute-start.2 = (f32[16,8,128]{2,1,0:T(8,128)S(1)}, f32[16,8,128]{2,1,0:T(8,128)S(1)}, u32[]{:S(2)}, u32[]{:S(2)}) collective-permute-start(f32[16,8,128]{2,1,0:T(8,128)S(1)} %get-tuple-element.58), channel_id=1, source_target_pairs={{0,4},{1,5},{2,6},{3,7},{4,0},{5,1},{6,2},{7,3},{8,12},{9,13},{10,... | collective-permute-start | bytes 196616 | tf_op jit(solution)/shard_map/ppermute | solution.py:12
  13.2 2.7 %collective-permute-start.3 = (f32[16,8,128]{2,1,0:T(8,128)S(1)}, f32[16,8,128]{2,1,0:T(8,128)S(1)}, u32[]{:S(2)}, u32[]{:S(2)}) collective-permute-start(f32[16,8,128]{2,1,0:T(8,128)S(1)} %get-tuple-element.56), channel_id=1, source_target_pairs={{0,8},{1,9},{2,10},{3,11},{4,12},{5,13},{6,14},{7,15},{8,0},{9,1},... | collective-permute-start | bytes 196616 | tf_op jit(solution)/shard_map/ppermute | solution.py:12
  15.9 0.8 copy.46
  16.8 0.9 copy.60
  17.7 0.8 broadcast_multiply_fusion
  20.7 2.4 %collective-permute-done.9 = f32[16,8,128]{2,1,0:T(8,128)S(1)} collective-permute-done((f32[16,8,128]{2,1,0:T(8,128)S(1)}, f32[16,8,128]{2,1,0:T(8,128)S(1)}, u32[]{:S(2)}, u32[]{:S(2)}) %collective-permute-start.9) | collective-permute-done | bytes 65568 | tf_op jit(solution)/shard_map/ppermute | solution.py:12
  23.1 1.1 collective-permute-done.10
  24.2 2.1 %collective-permute-done.11 = f32[16,8,128]{2,1,0:T(8,128)S(1)} collective-permute-done((f32[16,8,128]{2,1,0:T(8,128)S(1)}, f32[16,8,128]{2,1,0:T(8,128)S(1)}, u32[]{:S(2)}, u32[]{:S(2)}) %collective-permute-start.11) | collective-permute-done | bytes 65568 | tf_op jit(solution)/shard_map/ppermute | solution.py:12
  27.3 9.4 %convolution_bitcast_fusion.3 = f32[32,8,128]{2,1,0:T(8,128)S(1)} fusion(f32[32,4,8,128]{3,2,1,0:T(8,128)S(1)} %bitcast.106, f32[32,4,128,128]{3,2,1,0:T(8,128)} %param.15), kind=kOutput, calls=%fused_computation.24 | convolution fusion | flops 201326592 | bytes 9043968 | tf_op jit(solution)/shard_map/blij,blmj->bmi/dot_general | solution.py:24
  36.8 9.3 %convolution_bitcast_fusion.1 = f32[32,8,128]{2,1,0:T(8,128)S(1)} fusion(f32[32,4,8,128]{3,2,1,0:T(8,128)S(1)} %bitcast.104, f32[32,4,128,128]{3,2,1,0:T(8,128)} %param.15), kind=kOutput, calls=%fused_computation.22 | convolution fusion | flops 201326592 | bytes 9043968 | tf_op jit(solution)/shard_map/blij,blmj->bmi/dot_general | solution.py:24
  51.3 1.6 collective-permute-start.5
  53.3 1.5 collective-permute-start.7
  54.8 1.5 collective-permute-start.15
  56.3 1.8 %collective-permute-start.14 = (f32[16,8,128]{2,1,0:T(8,128)S(1)}, f32[16,8,128]{2,1,0:T(8,128)S(1)}, u32[]{:S(2)}, u32[]{:S(2)}) collective-permute-start(f32[16,8,128]{2,1,0:T(8,128)S(1)} %get-tuple-element.47), channel_id=1, source_target_pairs={{0,4},{1,5},{2,6},{3,7},{4,0},{5,1},{6,2},{7,3},{8,12},{9,13},{10,... | collective-permute-start | bytes 196616 | tf_op jit(solution)/shard_map/ppermute | solution.py:12
  58.9 3.0 %collective-permute-done.7 = f32[16,8,128]{2,1,0:T(8,128)S(1)} collective-permute-done((f32[16,8,128]{2,1,0:T(8,128)S(1)}, f32[16,8,128]{2,1,0:T(8,128)S(1)}, u32[]{:S(2)}, u32[]{:S(2)}) %collective-permute-start.7) | collective-permute-done | bytes 65568 | tf_op jit(solution)/shard_map/ppermute | solution.py:12
  62.8 0.8 gather_fusion.20
  63.8 9.3 %convolution_bitcast_fusion.2 = f32[32,8,128]{2,1,0:T(8,128)S(1)} fusion(f32[32,4,8,128]{3,2,1,0:T(8,128)S(1)} %bitcast.105, f32[32,4,128,128]{3,2,1,0:T(8,128)} %param.15), kind=kOutput, calls=%fused_computation.23 | convolution fusion | flops 201326592 | bytes 9043968 | tf_op jit(solution)/shard_map/blij,blmj->bmi/dot_general | solution.py:24
  73.1 9.5 %convolution_bitcast_fusion = f32[32,8,128]{2,1,0:T(8,128)S(1)} fusion(f32[32,4,8,128]{3,2,1,0:T(8,128)S(1)} %bitcast.103, f32[32,4,128,128]{3,2,1,0:T(8,128)} %param.15), kind=kOutput, calls=%fused_computation.21 | convolution fusion | flops 201326592 | bytes 9043968 | tf_op jit(solution)/shard_map/blij,blmj->bmi/dot_general | solution.py:24
  84.6 68.0 %gather_fusion = f32[12288]{0:T(1024)S(1)} fusion(f32[4096]{0:T(1024)S(1)} %fusion.13, s32[12288]{0:T(1024)S(1)} %broadcast_clamp_fusion), kind=kCustom, calls=%fused_computation.20 | custom fusion | bytes 147456 | tf_op jit(solution)/shard_map/jit(_take)/gather | solution.py:92
  152.7 4.9 %psum.7 = f32[1024]{0:T(1024)S(1)} all-reduce(f32[1024]{0:T(1024)S(1)} %broadcast_multiply_fusion.1), channel_id=1, replica_groups=mesh['freq'=2,'dom'=16] {'freq'}, use_global_device_ids=true, to_apply=%region_2.5 | all-reduce | flops 1024 | bytes 8192 | tf_op jit(solution)/shard_map/psum | solution.py:95
  (109 shorter events, 18.6 us)
Async XLA Ops:
  4.7 13.8 %collective-permute-start = (f32[16,8,128]{2,1,0:T(8,128)S(1)}, f32[16,8,128]{2,1,0:T(8,128)S(1)}, u32[]{:S(2)}, u32[]{:S(2)}) collective-permute-start(f32[16,8,128]{2,1,0:T(8,128)S(1)} %get-tuple-element.62), channel_id=1, source_target_pairs={{0,1},{1,0},{2,3},{3,2},{4,5},{5,4},{6,7},{7,6},{8,9},{9,8},{10,11... | collective-permute-start | bytes 196616 | tf_op jit(solution)/shard_map/ppermute | solution.py:12
  6.5 12.7 %collective-permute-start.1 = (f32[16,8,128]{2,1,0:T(8,128)S(1)}, f32[16,8,128]{2,1,0:T(8,128)S(1)}, u32[]{:S(2)}, u32[]{:S(2)}) collective-permute-start(f32[16,8,128]{2,1,0:T(8,128)S(1)} %get-tuple-element.60), channel_id=1, source_target_pairs={{0,2},{1,3},{2,0},{3,1},{4,6},{5,7},{6,4},{7,5},{8,10},{9,11},{10,... | collective-permute-start | bytes 196616 | tf_op jit(solution)/shard_map/ppermute | solution.py:12
  10.3 9.4 %collective-permute-start.2 = (f32[16,8,128]{2,1,0:T(8,128)S(1)}, f32[16,8,128]{2,1,0:T(8,128)S(1)}, u32[]{:S(2)}, u32[]{:S(2)}) collective-permute-start(f32[16,8,128]{2,1,0:T(8,128)S(1)} %get-tuple-element.58), channel_id=1, source_target_pairs={{0,4},{1,5},{2,6},{3,7},{4,0},{5,1},{6,2},{7,3},{8,12},{9,13},{10,... | collective-permute-start | bytes 196616 | tf_op jit(solution)/shard_map/ppermute | solution.py:12
  13.2 6.7 %collective-permute-start.3 = (f32[16,8,128]{2,1,0:T(8,128)S(1)}, f32[16,8,128]{2,1,0:T(8,128)S(1)}, u32[]{:S(2)}, u32[]{:S(2)}) collective-permute-start(f32[16,8,128]{2,1,0:T(8,128)S(1)} %get-tuple-element.56), channel_id=1, source_target_pairs={{0,8},{1,9},{2,10},{3,11},{4,12},{5,13},{6,14},{7,15},{8,0},{9,1},... | collective-permute-start | bytes 196616 | tf_op jit(solution)/shard_map/ppermute | solution.py:12
  15.8 4.8 %collective-permute-start.8 = (f32[16,8,128]{2,1,0:T(8,128)S(1)}, f32[16,8,128]{2,1,0:T(8,128)S(1)}, u32[]{:S(2)}, u32[]{:S(2)}) collective-permute-start(f32[16,8,128]{2,1,0:T(8,128)S(1)} %get-tuple-element.61), channel_id=1, source_target_pairs={{0,1},{1,0},{2,3},{3,2},{4,5},{5,4},{6,7},{7,6},{8,9},{9,8},{10,11... | collective-permute-start | bytes 196616 | tf_op jit(solution)/shard_map/ppermute | solution.py:12
  18.6 4.6 %collective-permute-start.9 = (f32[16,8,128]{2,1,0:T(8,128)S(1)}, f32[16,8,128]{2,1,0:T(8,128)S(1)}, u32[]{:S(2)}, u32[]{:S(2)}) collective-permute-start(f32[16,8,128]{2,1,0:T(8,128)S(1)} %get-tuple-element.59), channel_id=1, source_target_pairs={{0,2},{1,3},{2,0},{3,1},{4,6},{5,7},{6,4},{7,5},{8,10},{9,11},{10,... | collective-permute-start | bytes 196616 | tf_op jit(solution)/shard_map/ppermute | solution.py:12
  19.2 5.0 %collective-permute-start.10 = (f32[16,8,128]{2,1,0:T(8,128)S(1)}, f32[16,8,128]{2,1,0:T(8,128)S(1)}, u32[]{:S(2)}, u32[]{:S(2)}) collective-permute-start(f32[16,8,128]{2,1,0:T(8,128)S(1)} %get-tuple-element.57), channel_id=1, source_target_pairs={{0,4},{1,5},{2,6},{3,7},{4,0},{5,1},{6,2},{7,3},{8,12},{9,13},{10,... | collective-permute-start | bytes 196616 | tf_op jit(solution)/shard_map/ppermute | solution.py:12
  19.7 6.6 %collective-permute-start.11 = (f32[16,8,128]{2,1,0:T(8,128)S(1)}, f32[16,8,128]{2,1,0:T(8,128)S(1)}, u32[]{:S(2)}, u32[]{:S(2)}) collective-permute-start(f32[16,8,128]{2,1,0:T(8,128)S(1)} %get-tuple-element.55), channel_id=1, source_target_pairs={{0,8},{1,9},{2,10},{3,11},{4,12},{5,13},{6,14},{7,15},{8,0},{9,1},... | collective-permute-start | bytes 196616 | tf_op jit(solution)/shard_map/ppermute | solution.py:12
  27.3 18.8 %copy-start = (f32[2,4,32,128]{3,2,1,0:T(8,128)S(1)}, f32[2,4,32,128]{3,2,1,0:T(8,128)}, u32[]{:S(2)}) copy-start(f32[2,4,32,128]{3,2,1,0:T(8,128)} %param.14) | copy-start | bytes 393220
  27.3 18.8 %copy-start.1 = (f32[2,4,32,128]{3,2,1,0:T(8,128)S(1)}, f32[2,4,32,128]{3,2,1,0:T(8,128)}, u32[]{:S(2)}) copy-start(f32[2,4,32,128]{3,2,1,0:T(8,128)} %param.13) | copy-start | bytes 393220
  51.1 5.2 %collective-permute-start.4 = (f32[16,8,128]{2,1,0:T(8,128)S(1)}, f32[16,8,128]{2,1,0:T(8,128)S(1)}, u32[]{:S(2)}, u32[]{:S(2)}) collective-permute-start(f32[16,8,128]{2,1,0:T(8,128)S(1)} %get-tuple-element.52), channel_id=1, source_target_pairs={{0,1},{1,0},{2,3},{3,2},{4,5},{5,4},{6,7},{7,6},{8,9},{9,8},{10,11... | collective-permute-start | bytes 196616 | tf_op jit(solution)/shard_map/ppermute | solution.py:12
  51.3 6.8 %collective-permute-start.5 = (f32[16,8,128]{2,1,0:T(8,128)S(1)}, f32[16,8,128]{2,1,0:T(8,128)S(1)}, u32[]{:S(2)}, u32[]{:S(2)}) collective-permute-start(f32[16,8,128]{2,1,0:T(8,128)S(1)} %get-tuple-element.50), channel_id=1, source_target_pairs={{0,2},{1,3},{2,0},{3,1},{4,6},{5,7},{6,4},{7,5},{8,10},{9,11},{10,... | collective-permute-start | bytes 196616 | tf_op jit(solution)/shard_map/ppermute | solution.py:12
  53.0 5.8 %collective-permute-start.6 = (f32[16,8,128]{2,1,0:T(8,128)S(1)}, f32[16,8,128]{2,1,0:T(8,128)S(1)}, u32[]{:S(2)}, u32[]{:S(2)}) collective-permute-start(f32[16,8,128]{2,1,0:T(8,128)S(1)} %get-tuple-element.48), channel_id=1, source_target_pairs={{0,4},{1,5},{2,6},{3,7},{4,0},{5,1},{6,2},{7,3},{8,12},{9,13},{10,... | collective-permute-start | bytes 196616 | tf_op jit(solution)/shard_map/ppermute | solution.py:12
  53.3 8.6 %collective-permute-start.7 = (f32[16,8,128]{2,1,0:T(8,128)S(1)}, f32[16,8,128]{2,1,0:T(8,128)S(1)}, u32[]{:S(2)}, u32[]{:S(2)}) collective-permute-start(f32[16,8,128]{2,1,0:T(8,128)S(1)} %get-tuple-element.46), channel_id=1, source_target_pairs={{0,8},{1,9},{2,10},{3,11},{4,12},{5,13},{6,14},{7,15},{8,0},{9,1},... | collective-permute-start | bytes 196616 | tf_op jit(solution)/shard_map/ppermute | solution.py:12
  54.8 7.9 %collective-permute-start.15 = (f32[16,8,128]{2,1,0:T(8,128)S(1)}, f32[16,8,128]{2,1,0:T(8,128)S(1)}, u32[]{:S(2)}, u32[]{:S(2)}) collective-permute-start(f32[16,8,128]{2,1,0:T(8,128)S(1)} %get-tuple-element.45), channel_id=1, source_target_pairs={{0,8},{1,9},{2,10},{3,11},{4,12},{5,13},{6,14},{7,15},{8,0},{9,1},... | collective-permute-start | bytes 196616 | tf_op jit(solution)/shard_map/ppermute | solution.py:12
  56.3 6.4 %collective-permute-start.14 = (f32[16,8,128]{2,1,0:T(8,128)S(1)}, f32[16,8,128]{2,1,0:T(8,128)S(1)}, u32[]{:S(2)}, u32[]{:S(2)}) collective-permute-start(f32[16,8,128]{2,1,0:T(8,128)S(1)} %get-tuple-element.47), channel_id=1, source_target_pairs={{0,4},{1,5},{2,6},{3,7},{4,0},{5,1},{6,2},{7,3},{8,12},{9,13},{10,... | collective-permute-start | bytes 196616 | tf_op jit(solution)/shard_map/ppermute | solution.py:12
  58.2 4.6 %collective-permute-start.13 = (f32[16,8,128]{2,1,0:T(8,128)S(1)}, f32[16,8,128]{2,1,0:T(8,128)S(1)}, u32[]{:S(2)}, u32[]{:S(2)}) collective-permute-start(f32[16,8,128]{2,1,0:T(8,128)S(1)} %get-tuple-element.49), channel_id=1, source_target_pairs={{0,2},{1,3},{2,0},{3,1},{4,6},{5,7},{6,4},{7,5},{8,10},{9,11},{10,... | collective-permute-start | bytes 196616 | tf_op jit(solution)/shard_map/ppermute | solution.py:12
  58.8 3.9 %collective-permute-start.12 = (f32[16,8,128]{2,1,0:T(8,128)S(1)}, f32[16,8,128]{2,1,0:T(8,128)S(1)}, u32[]{:S(2)}, u32[]{:S(2)}) collective-permute-start(f32[16,8,128]{2,1,0:T(8,128)S(1)} %get-tuple-element.51), channel_id=1, source_target_pairs={{0,1},{1,0},{2,3},{3,2},{4,5},{5,4},{6,7},{7,6},{8,9},{9,8},{10,11... | collective-permute-start | bytes 196616 | tf_op jit(solution)/shard_map/ppermute | solution.py:12
  73.0 11.4 %copy-start.4 = (f32[2]{0:T(128)S(1)}, f32[2]{0:T(128)}, u32[]{:S(2)}) copy-start(f32[2]{0:T(128)} %param.19) | copy-start | bytes 28
  84.5 68.1 %copy-start.2 = (s32[12,1024]{1,0:T(8,128)S(1)}, s32[12,1024]{1,0:T(8,128)}, u32[]{:S(2)}) copy-start(s32[12,1024]{1,0:T(8,128)} %param.20) | copy-start | bytes 147460
  84.5 73.1 %copy-start.3 = (f32[1024]{0:T(1024)S(1)}, f32[1024]{0:T(1024)}, u32[]{:S(2)}) copy-start(f32[1024]{0:T(1024)} %param.21) | copy-start | bytes 12292
where the time goes:
time: 159 us; the launch traced here: 158 us
  local copies, waits for them, and re-layouts  84.3 us (53%)
  matrix products  37.4 us (24%)
  starting transfers between devices  16 us (10%)
  waiting for transfers between devices  8.71 us (5%)
  other arithmetic  5.52 us (3%)
  blocking collectives  4.95 us (3%)
    gather x2, local copies, waits for them, and re-layouts, local(): jnp.take(edge_term, cell_edges.reshape(-1), axis=0)  68 us
    dot_general x4, matrix products, operate(): jnp.einsum('blij,blmj->bmi', curl_blocks, gathered, precision=lax.Precisi...  37.4 us
    ppermute x16, starting transfers between devices, swapped(): return lax.ppermute(value, axis, pairs)  16 us
    gather x16, local copies, waits for them, and re-layouts, operate(): outgoing = jnp.take(field, tile_lists[bit], axis=0)  9.04 us
    ppermute x16, waiting for transfers between devices, swapped(): return lax.ppermute(value, axis, pairs)  8.71 us
    psum x1, blocking collectives, local(): grad = lax.psum(partial_grad, 'freq')  4.95 us
  transfers between devices with their start and end apart: 16, of which 4 were waited for; matrix products, arithmetic and copies ran while one was open for 5% of the time, Pallas kernels for 0%

commit v1 on v0

v1 whole, which is shorter than its diff:
```python
import functools

import jax
import jax.numpy as jnp
from jax import lax
from jax.experimental import pallas as pl
from jax.experimental.pallas import tpu as pltpu
from jax.sharding import PartitionSpec as P

THETA = 1.0
DELTA = 0.7
MESH = pl.DeviceIdType.MESH
CHUNK = 4
UNROLL = 4


def chebyshev_factors():
    sone = THETA / DELTA
    rho = 1.0 / sone
    factors = []
    for _ in range(2):
        rho_new = 1.0 / (2.0 * sone - rho)
        factors.append((rho_new * rho, 2.0 * rho_new / DELTA))
        rho = rho_new
    return factors


def split(value):
    high = value.astype(jnp.bfloat16)
    low = (value - high.astype(jnp.float32)).astype(jnp.bfloat16)
    return high, low


def row_of(count, system, f, c):
    return (c % 2) * 4 * count + system * 2 * count + f * 2 + c // 2


def kernel(
    peers,
    links_ref,
    tiles_ref,
    omega_ref,
    fwd_ref,
    adj_ref,
    curl_ref,
    mass_ref,
    total,
    edge_out,
    raw,
    parts,
    first,
    second,
    resid,
    ext_one,
    ext_two,
    send_one,
    send_two,
    terms,
    raw_sem,
    send_sem,
    recv_sem,
    term_send_sem,
    term_recv_sem,
):
    blocks = mass_ref.shape[0]
    count = fwd_ref.shape[0]
    width = 8 * count
    half = width // 2
    rounds, tiles = tiles_ref.shape
    links = links_ref.shape[1]
    size = mass_ref.shape[1]
    freq = lax.axis_index("freq")
    dom = lax.axis_index("dom")

    def raw_copy(chunk):
        rows = pl.ds(chunk * CHUNK, CHUNK)
        return pltpu.make_async_copy(curl_ref.at[rows], raw.at[rows], raw_sem.at[chunk])

    for chunk in range(blocks // CHUNK):
        raw_copy(chunk).start()

    partners = []
    for bit in range(rounds):
        mask = 2**bit
        partners.append((freq, dom + mask * (1 - 2 * ((dom // mask) % 2))))
    others = [(lax.rem(freq + step, peers), dom) for step in range(1, peers)]

    barrier = pltpu.get_barrier_semaphore()
    for device in partners + others:
        pl.semaphore_signal(barrier, inc=1, device_id=device, device_id_type=MESH)

    for system, ref in enumerate((fwd_ref, adj_ref)):
        for f in range(count):
            for c in range(4):
                first[:, row_of(count, system, f, c), :] = ref[f, c]

    def exchange(field, send, ext, phase):
        copies = []
        for bit in reversed(range(rounds)):
            for tile in range(tiles):
                send[bit * tiles + tile] = field[tiles_ref[bit, tile]]
            if phase == 0 and bit == rounds - 1:
                pl.semaphore_wait(barrier, len(partners) + len(others))
            copy = pltpu.make_async_remote_copy(
                src_ref=send.at[pl.ds(bit * tiles, tiles)],
                dst_ref=ext.at[pl.ds(blocks + bit * tiles, tiles)],
                send_sem=send_sem.at[phase, bit],
                recv_sem=recv_sem.at[phase, bit],
                device_id=partners[bit],
                device_id_type=MESH,
            )
            copy.start()
            copies.append(copy)
        return copies

    copies = exchange(first, send_one, ext_one, 0)
    ext_one[pl.ds(0, blocks)] = first[...]

    for chunk in range(blocks // CHUNK):
        raw_copy(chunk).wait()

        def cut(step, carry):
            row = chunk * CHUNK + step
            for link in range(links):
                high, low = split(raw[row, link])
                columns = pl.ds(link * size, size)
                parts[row, pl.ds(0, size), columns] = high
                parts[row, pl.ds(size, size), columns] = low
            return carry

        lax.fori_loop(0, CHUNK, cut, 0)

    place = lax.broadcasted_iota(jnp.int32, (half, size), 0)
    place = lax.rem(place // 2, count)
    omega = jnp.zeros((half, size), jnp.float32)
    for f in range(count):
        omega = jnp.where(place == f, omega_ref[f], omega)

    def operate(row, field, ext):
        gathered = [ext[links_ref[row, link]] for link in range(links)]
        high, low = split(jnp.concatenate(gathered, axis=1))
        both = jnp.concatenate([high, low], axis=0)
        product = lax.dot_general(
            both, parts[row], (((1,), (1,)), ((), ())), preferred_element_type=jnp.float32
        )
        product = product[:width] + product[width:]
        curl = product[:, :size] + product[:, size:]
        weight = omega * mass_ref[pl.ds(row, 1), :]
        real = field[row, pl.ds(0, half)]
        imag = field[row, pl.ds(half, half)]
        return real, imag, curl[:half] - weight * imag, curl[half:] + weight * real

    factors = chebyshev_factors()

    for copy in copies:
        copy.wait()

    def one(step, carry):
        keep, gain = factors[0]
        for inner in range(UNROLL):
            row = step * UNROLL + inner
            real, imag, image_real, image_imag = operate(row, first, ext_one)
            for value, image, start in ((real, image_real, 0), (imag, image_imag, half)):
                left = value - image
                resid[row, pl.ds(start, half)] = left
                second[row, pl.ds(start, half)] = keep * value + gain * left
        return carry

    lax.fori_loop(0, blocks // UNROLL, one, 0)

    copies = exchange(second, send_two, ext_two, 1)
    ext_two[pl.ds(0, blocks)] = second[...]
    for copy in copies:
        copy.wait()

    def two(step, carry):
        keep, gain = factors[1]
        for inner in range(UNROLL):
            row = step * UNROLL + inner
            real, imag, image_real, image_imag = operate(row, second, ext_two)
            done = []
            for value, image, start in ((real, image_real, 0), (imag, image_imag, half)):
                left = resid[row, pl.ds(start, half)] - image
                step_three = keep * value + gain * left
                done.append((first[row, pl.ds(start, half)] + value) + step_three)
                total[row, pl.ds(start, half)] = done[-1]
            crossed = jnp.concatenate([done[1][half // 2 :], done[1][: half // 2]], axis=0)
            term = omega * done[0] * crossed
            terms[freq, pl.ds(row, 1), :] = jnp.sum(term, axis=0, keepdims=True)
        return carry

    lax.fori_loop(0, blocks // UNROLL, two, 0)

    copies = []
    for step in range(1, peers):
        copy = pltpu.make_async_remote_copy(
            src_ref=terms.at[freq],
            dst_ref=terms.at[freq],
            send_sem=term_send_sem.at[step],
            recv_sem=term_recv_sem.at[step],
            device_id=others[step - 1],
            device_id_type=MESH,
        )
        copy.start()
        copies.append(copy)
    for copy in copies:
        copy.wait()
    whole = terms[0]
    for peer in range(1, peers):
        whole = whole + terms[peer]
    edge_out[...] = whole


def finish(scale, total_ref, edge_ref, cells_ref, cond_ref, fwd_out, adj_out, model_out):
    blocks, size = edge_ref.shape
    count = fwd_out.shape[0]
    width = 8 * count
    for system, ref in enumerate((fwd_out, adj_out)):
        for f in range(count):
            for c in range(4):
                row = row_of(count, system, f, c)
                ref[f, c] = total_ref[:, row, :]

    corners, cells = cells_ref.shape
    shift = size.bit_length() - 1
    sums = []
    for column in range(cells // size):
        acc = jnp.zeros((1, size), jnp.float32)
        for start in range(0, corners, 8):
            rows = min(8, corners - start)
            ids = cells_ref[pl.ds(start, rows), pl.ds(column * size, size)]
            if rows < 8:
                ids = jnp.concatenate([ids, jnp.full((8 - rows, size), -1, jnp.int32)], axis=0)
            block = ids >> shift
            lane = ids & (size - 1)
            found = jnp.zeros((8, size), jnp.float32)
            for row in range(blocks):
                values = jnp.broadcast_to(edge_ref[pl.ds(row, 1), :], (8, size))
                got = jnp.take_along_axis(values, lane, axis=1, mode="promise_in_bounds")
                found = jnp.where(block == row, got, found)
            acc = acc + jnp.sum(found, axis=0, keepdims=True)
        sums.append(acc)
    grad = jnp.concatenate(sums, axis=0) * scale
    model_out[...] = cond_ref[...] - 0.5 * grad / jnp.sqrt(grad * grad + 1.0)


def local(
    fwd_source,
    adj_source,
    curl_blocks,
    block_links,
    tile_lists,
    edge_mass,
    omega,
    cell_edges,
    log_cond,
):
    count, _, blocks, size = fwd_source.shape
    peers = lax.axis_size("freq")
    width = 8 * count
    rounds, tiles = tile_lists.shape
    sent = rounds * tiles
    links = block_links.shape[1]
    cells = log_cond.shape[0]
    cond = log_cond.reshape(cells // size, size)
    f32, bf16 = jnp.float32, jnp.bfloat16
    vmem = pl.BlockSpec(memory_space=pltpu.VMEM)
    smem = pl.BlockSpec(memory_space=pltpu.SMEM)
    total, edge = pl.pallas_call(
        functools.partial(kernel, peers),
        out_shape=(
            jax.ShapeDtypeStruct((blocks, width, size), f32),
            jax.ShapeDtypeStruct((blocks, size), f32),
        ),
        in_specs=[smem, smem, smem, vmem, vmem, pl.BlockSpec(memory_space=pl.ANY), vmem],
        out_specs=(vmem, vmem),
        scratch_shapes=[
            pltpu.VMEM(curl_blocks.shape, f32),
            pltpu.VMEM((blocks, 2 * size, links * size), bf16),
            pltpu.VMEM((blocks, width, size), f32),
            pltpu.VMEM((blocks, width, size), f32),
            pltpu.VMEM((blocks, width, size), f32),
            pltpu.VMEM((blocks + sent, width, size), f32),
            pltpu.VMEM((blocks + sent, width, size), f32),
            pltpu.VMEM((sent, width, size), f32),
            pltpu.VMEM((sent, width, size), f32),
            pltpu.VMEM((peers, blocks, size), f32),
            pltpu.SemaphoreType.DMA((blocks // CHUNK,)),
            pltpu.SemaphoreType.DMA((2, rounds)),
            pltpu.SemaphoreType.DMA((2, rounds)),
            pltpu.SemaphoreType.DMA((peers,)),
            pltpu.SemaphoreType.DMA((peers,)),
        ],
        compiler_params=pltpu.CompilerParams(
            collective_id=0, has_side_effects=True, vmem_limit_bytes=48 * 1024 * 1024
        ),
    )(block_links, tile_lists, omega, fwd_source, adj_source, curl_blocks, edge_mass)
    scale = 1.0 / (24.0 * count * peers) ** 0.5
    fwd_field, adj_field, model = pl.pallas_call(
        functools.partial(finish, scale),
        out_shape=(
            jax.ShapeDtypeStruct(fwd_source.shape, f32),
            jax.ShapeDtypeStruct(adj_source.shape, f32),
            jax.ShapeDtypeStruct(cond.shape, f32),
        ),
        in_specs=[vmem] * 4,
        out_specs=(vmem,) * 3,
    )(total, edge, cell_edges, cond)
    return fwd_field, adj_field, model.reshape(cells)


def solution(mesh):
    in_specs = (
        P("freq", None, "dom", None),
        P("freq", None, "dom", None),
        P("dom", None, None, None),
        P("dom", None),
        P("dom", None),
        P("dom", None),
        P("freq"),
        P(None, "dom"),
        P("dom"),
    )
    out_specs = (P("freq", None, "dom", None), P("freq", None, "dom", None), P("dom"))
    return jax.shard_map(local, mesh=mesh, in_specs=in_specs, out_specs=out_specs, check_vma=False)
```

time: 159 us -> 39.3 us (0.25)
  local copies, waits for them, and re-layouts: 84.3 us -> 5.9 us
  matrix products: 37.4 us -> 0 us
  Pallas kernels: 0 us -> 32.5 us
  starting transfers between devices: 16 us -> 0 us
  waiting for transfers between devices: 8.71 us -> 0 us
  other arithmetic: 5.52 us -> 0 us
  blocking collectives: 4.95 us -> 0 us
    gather x22 -> x0, local copies, waits for them, and re-layouts: 80.1 us -> none  [the longest x2 68 us: local(): jnp.take(edge_term, cell_edges.reshape(-1), axis=0)]
    dot_general x4 -> x0, matrix products: 37.4 us -> none  [operate(): jnp.einsum('blij,blmj->bmi', curl_blocks, gathered, precision=lax.Precisi...]
    pallas_call x0 -> x2, Pallas kernels: none -> 32.5 us  [the longest x1 30.1 us: local(): pl.pallas_call(functools.partial(kernel, peers), out_shape=(jax.ShapeDtyp...]
    ppermute x16 -> x0, starting transfers between devices: 16 us -> none  [swapped(): return lax.ppermute(value, axis, pairs)]
    ppermute x16 -> x0, waiting for transfers between devices: 8.71 us -> none  [swapped(): return lax.ppermute(value, axis, pairs)]
    psum x1 -> x0, blocking collectives: 4.95 us -> none  [local(): grad = lax.psum(partial_grad, 'freq')]
    unnamed x26 -> x15, local copies, waits for them, and re-layouts: 1.78 us -> 5.9 us
    transpose x2 -> x0, local copies, waits for them, and re-layouts: 1.99 us -> none  [to_rows(): moved = jnp.transpose(fields, (3, 0, 1, 2, 4))]
  transfers between devices with their start and end apart: 16 -> 0, of which waited for: 4 -> 0; matrix products, arithmetic and copies ran while one was open for 5% -> 0% of each run, Pallas kernels for 0% -> 0%
where the time goes in v1:
time: 39.3 us; the launch traced here: 39 us
  Pallas kernels  32.5 us (83%)
  local copies, waits for them, and re-layouts  5.9 us (15%)
  between operations  0.65 us (2%)
    pallas_call x1, Pallas kernels, local(): pl.pallas_call(functools.partial(kernel, peers), out_shape=(jax.ShapeDtyp...  30.1 us
    unnamed x15, local copies, waits for them, and re-layouts  5.9 us
    pallas_call x1, Pallas kernels, local(): pl.pallas_call(functools.partial(finish, scale), out_shape=(jax.ShapeDtyp...  2.37 us

profile of v1, /device:TPU:0, one launch (start us, length us, event | category | flops | bytes accessed | tf_op | source)
XLA Modules:
  0.0 39.0 jit_solution(14082300484967044219)
XLA Ops:
  0.6 0.8 %copy.12.links_ref = s32[32,4]{1,0:T(8,128)S(1)} copy(s32[32,4]{0,1:T(4,128)} %param.12) | data formatting | bytes 1024 | tf_op args[3]
  1.4 0.0 copy-start.1
  1.4 0.9 %copy-done.1 = f32[2,4,32,128]{3,2,1,0:T(8,128)S(1)} copy-done((f32[2,4,32,128]{3,2,1,0:T(8,128)S(1)}, f32[2,4,32,128]{3,2,1,0:T(8,128)}, u32[]{:S(2)}) %copy-start.1) | copy-done | bytes 131096
  2.3 0.0 copy-start.2
  2.3 0.9 %copy-done.2 = f32[2,4,32,128]{3,2,1,0:T(8,128)S(1)} copy-done((f32[2,4,32,128]{3,2,1,0:T(8,128)S(1)}, f32[2,4,32,128]{3,2,1,0:T(8,128)}, u32[]{:S(2)}) %copy-start.2) | copy-done | bytes 131096
  3.2 0.0 copy-start.3
  3.2 0.7 %copy-done.3 = f32[32,128]{1,0:T(8,128)S(1)} copy-done((f32[32,128]{1,0:T(8,128)S(1)}, f32[32,128]{1,0:T(8,128)}, u32[]{:S(2)}) %copy-start.3) | copy-done | bytes 16408
  3.9 0.0 copy-start.5
  3.9 0.7 %copy-done.5 = s32[4,16]{1,0:T(4,128)S(1)} copy-done((s32[4,16]{1,0:T(4,128)S(1)}, s32[4,16]{1,0:T(4,128)}, u32[]{:S(2)}) %copy-start.5) | copy-done | bytes 280
  4.6 0.0 copy-start.6
  4.6 0.7 %copy-done.6 = f32[2]{0:T(128)S(1)} copy-done((f32[2]{0:T(128)S(1)}, f32[2]{0:T(128)}, u32[]{:S(2)}) %copy-start.6) | copy-done | bytes 32
  5.3 30.1 %shard_map.112 = (f32[32,16,128]{2,1,0:T(8,128)S(1)}, f32[32,128]{1,0:T(8,128)S(1)}) custom-call(s32[32,4]{1,0:T(8,128)S(1)} %copy.12.links_ref, s32[4,16]{1,0:T(4,128)S(1)} %copy-done.5, f32[2]{0:T(128)S(1)} %copy-done.6, f32[2,4,32,128]{3,2,1,0:T(8,128)S(1)} %copy-done.1, f32[2,4,32,128]{3,2,1,0:T(8,128)S(1)} %copy-done.2, f32[32,4,128,128]{3,2,1,0:T(8,128)} %curl_ref.1, ...), custom_call_target="tpu_custom_call" | custom-call | tf_op jit(solution)/shard_map/pallas_call | solution.py:269
  35.3 0.0 copy-start
  35.4 0.7 %copy-done = f32[32,16,128]{2,1,0:T(8,128)} copy-done((f32[32,16,128]{2,1,0:T(8,128)}, f32[32,16,128]{2,1,0:T(8,128)S(1)}, u32[]{:S(2)}) %copy-start) | copy-done | bytes 262168
  36.0 0.0 copy-start.4
  36.0 0.6 %copy-done.4 = f32[32,128]{1,0:T(8,128)} copy-done((f32[32,128]{1,0:T(8,128)}, f32[32,128]{1,0:T(8,128)S(1)}, u32[]{:S(2)}) %copy-start.4) | copy-done | bytes 16408
  36.6 2.4 %shard_map.113 = (f32[2,4,32,128]{3,2,1,0:T(8,128)}, f32[2,4,32,128]{3,2,1,0:T(8,128)}, f32[8,128]{1,0:T(8,128)}) custom-call(f32[32,16,128]{2,1,0:T(8,128)} %copy-done, f32[32,128]{1,0:T(8,128)} %copy-done.4, s32[12,1024]{1,0:T(8,128)} %cells_ref.1, f32[8,128]{1,0:T(8,128)} %bitcast.2), custom_call_target="tpu_custom_call" | custom-call | tf_op jit(solution)/shard_map/pallas_call | solution.py:299
Async XLA Ops:
  1.4 0.9 %copy-start.1 = (f32[2,4,32,128]{3,2,1,0:T(8,128)S(1)}, f32[2,4,32,128]{3,2,1,0:T(8,128)}, u32[]{:S(2)}) copy-start(f32[2,4,32,128]{3,2,1,0:T(8,128)} %fwd_ref.1) | copy-start | bytes 393220
  2.3 0.9 %copy-start.2 = (f32[2,4,32,128]{3,2,1,0:T(8,128)S(1)}, f32[2,4,32,128]{3,2,1,0:T(8,128)}, u32[]{:S(2)}) copy-start(f32[2,4,32,128]{3,2,1,0:T(8,128)} %adj_ref.1) | copy-start | bytes 393220
  3.2 0.7 %copy-start.3 = (f32[32,128]{1,0:T(8,128)S(1)}, f32[32,128]{1,0:T(8,128)}, u32[]{:S(2)}) copy-start(f32[32,128]{1,0:T(8,128)} %mass_ref.1) | copy-start | bytes 49156
  3.9 0.7 %copy-start.5 = (s32[4,16]{1,0:T(4,128)S(1)}, s32[4,16]{1,0:T(4,128)}, u32[]{:S(2)}) copy-start(s32[4,16]{1,0:T(4,128)} %tiles_ref.1) | copy-start | bytes 772
  4.6 0.7 %copy-start.6 = (f32[2]{0:T(128)S(1)}, f32[2]{0:T(128)}, u32[]{:S(2)}) copy-start(f32[2]{0:T(128)} %omega_ref.1) | copy-start | bytes 28
  35.3 0.7 %copy-start = (f32[32,16,128]{2,1,0:T(8,128)}, f32[32,16,128]{2,1,0:T(8,128)S(1)}, u32[]{:S(2)}) copy-start(f32[32,16,128]{2,1,0:T(8,128)S(1)} %get-tuple-element.8.total_ref) | copy-start | bytes 786436
  36.0 0.6 %copy-start.4 = (f32[32,128]{1,0:T(8,128)}, f32[32,128]{1,0:T(8,128)S(1)}, u32[]{:S(2)}) copy-start(f32[32,128]{1,0:T(8,128)S(1)} %get-tuple-element.9.edge_ref) | copy-start | bytes 49156

commit v2 on v1

v2 whole, which is shorter than its diff:
```python
import functools

import jax
import jax.numpy as jnp
from jax import lax
from jax.experimental import pallas as pl
from jax.experimental.pallas import tpu as pltpu
from jax.sharding import PartitionSpec as P

THETA = 1.0
DELTA = 0.7
MESH = pl.DeviceIdType.MESH
VMEM = 63 * 1024 * 1024
CHUNK = 4
UNROLL = 4


def chebyshev_factors():
    sone = THETA / DELTA
    rho = 1.0 / sone
    factors = []
    for _ in range(2):
        rho_new = 1.0 / (2.0 * sone - rho)
        factors.append((rho_new * rho, 2.0 * rho_new / DELTA))
        rho = rho_new
    return factors


def split(value):
    high = value.astype(jnp.bfloat16)
    low = (value - high.astype(jnp.float32)).astype(jnp.bfloat16)
    return high, low


def row_of(count, system, f, c):
    return (c % 2) * 4 * count + system * 2 * count + f * 2 + c // 2


def kernel(
    peers,
    links_hbm,
    tiles_hbm,
    omega_hbm,
    fwd_hbm,
    adj_hbm,
    curl_hbm,
    mass_hbm,
    fwd_out,
    adj_out,
    edge_out,
    links_ref,
    tiles_ref,
    omega_ref,
    fwd_ref,
    adj_ref,
    mass_ref,
    raw,
    parts,
    weight,
    first,
    second,
    resid,
    total,
    ext_one,
    ext_two,
    send_one,
    send_two,
    terms,
    load_sem,
    raw_sem,
    send_sem,
    recv_sem,
    term_send_sem,
    term_recv_sem,
):
    blocks, size = mass_ref.shape
    count = fwd_ref.shape[0]
    width = 8 * count
    half = width // 2
    rounds, tiles = tiles_ref.shape
    links = links_ref.shape[0]
    freq = lax.axis_index("freq")
    dom = lax.axis_index("dom")

    loads = {}
    for at, (name, source, target) in enumerate(
        (
            ("fwd", fwd_hbm, fwd_ref),
            ("adj", adj_hbm, adj_ref),
            ("tiles", tiles_hbm, tiles_ref),
            ("links", links_hbm, links_ref),
            ("omega", omega_hbm, omega_ref),
            ("mass", mass_hbm, mass_ref),
        )
    ):
        loads[name] = pltpu.make_async_copy(source, target, load_sem.at[at])
        loads[name].start()

    def raw_copy(chunk):
        rows = pl.ds(chunk * CHUNK, CHUNK)
        return pltpu.make_async_copy(curl_hbm.at[rows], raw.at[rows], raw_sem.at[chunk])

    for chunk in range(blocks // CHUNK):
        raw_copy(chunk).start()

    partners = []
    for bit in range(rounds):
        mask = 2**bit
        partners.append((freq, dom + mask * (1 - 2 * ((dom // mask) % 2))))
    others = [(lax.rem(freq + step, peers), dom) for step in range(1, peers)]

    barrier = pltpu.get_barrier_semaphore()
    for device in partners + others:
        pl.semaphore_signal(barrier, inc=1, device_id=device, device_id_type=MESH)

    for system, (name, ref) in enumerate((("fwd", fwd_ref), ("adj", adj_ref))):
        loads[name].wait()
        for f in range(count):
            for c in range(4):
                first[:, row_of(count, system, f, c), :] = ref[f, c]

    pieces = 2
    span = tiles // pieces

    def push(send, ext, phase, bit, piece):
        rows = bit * tiles + piece * span
        copy = pltpu.make_async_remote_copy(
            src_ref=send.at[pl.ds(rows, span)],
            dst_ref=ext.at[pl.ds(blocks + rows, span)],
            send_sem=send_sem.at[phase, bit, piece],
            recv_sem=recv_sem.at[phase, bit, piece],
            device_id=partners[bit],
            device_id_type=MESH,
        )
        copy.start()
        return copy

    loads["tiles"].wait()
    copies = []
    for bit in reversed(range(rounds)):
        for piece in range(pieces):
            for tile in range(piece * span, (piece + 1) * span):
                send_one[bit * tiles + tile] = first[tiles_ref[bit, tile]]
            if len(copies) == 0:
                pl.semaphore_wait(barrier, len(partners) + len(others))
            copies.append(push(send_one, ext_one, 0, bit, piece))
    ext_one[pl.ds(0, blocks)] = first[...]

    for name in ("links", "omega", "mass"):
        loads[name].wait()
    place = lax.broadcasted_iota(jnp.int32, (half, size), 0)
    place = lax.rem(place // 2, count)
    omega = jnp.zeros((half, size), jnp.float32)
    for f in range(count):
        omega = jnp.where(place == f, omega_ref[f], omega)
    for row in range(blocks):
        weight[row] = omega * mass_ref[pl.ds(row, 1), :]

    for chunk in range(blocks // CHUNK):
        raw_copy(chunk).wait()

        def cut(step, carry):
            row = chunk * CHUNK + step
            for link in range(links):
                high, low = split(raw[row, link])
                columns = pl.ds(link * size, size)
                parts[row, pl.ds(0, size), columns] = high
                parts[row, pl.ds(size, size), columns] = low
            return carry

        lax.fori_loop(0, CHUNK, cut, 0)

    def operate(row, field, ext):
        gathered = [ext[links_ref[link, row]] for link in range(links)]
        high, low = split(jnp.concatenate(gathered, axis=1))
        both = jnp.concatenate([high, low], axis=0)
        product = lax.dot_general(
            both, parts[row], (((1,), (1,)), ((), ())), preferred_element_type=jnp.float32
        )
        product = product[:width] + product[width:]
        curl = product[:, :size] + product[:, size:]
        value = field[row]
        turned = jnp.concatenate([-value[half:], value[:half]], axis=0)
        scale = weight[row]
        return value, curl + jnp.concatenate([scale, scale], axis=0) * turned

    factors = chebyshev_factors()

    def advance(row):
        keep, gain = factors[0]
        value, image = operate(row, first, ext_one)
        left = value - image
        return left, keep * value + gain * left

    for copy in copies:
        copy.wait()

    copies = []
    for bit in reversed(range(rounds)[-2:]):
        for piece in range(pieces):

            def ahead(step, carry):
                for inner in range(UNROLL):
                    tile = piece * span + step * UNROLL + inner
                    send_two[bit * tiles + tile] = advance(tiles_ref[bit, tile])[1]
                return carry

            lax.fori_loop(0, span // UNROLL, ahead, 0)
            copies.append(push(send_two, ext_two, 1, bit, piece))

    def one(step, carry):
        for inner in range(UNROLL):
            row = step * UNROLL + inner
            left, value = advance(row)
            resid[row] = left
            second[row] = value
        return carry

    lax.fori_loop(0, blocks // UNROLL, one, 0)
    for bit in reversed(range(rounds)[:-2]):
        for piece in range(pieces):
            for tile in range(piece * span, (piece + 1) * span):
                send_two[bit * tiles + tile] = second[tiles_ref[bit, tile]]
            copies.append(push(send_two, ext_two, 1, bit, piece))
    ext_two[pl.ds(0, blocks)] = second[...]
    for copy in copies:
        copy.wait()

    def two(step, carry):
        keep, gain = factors[1]
        for inner in range(UNROLL):
            row = step * UNROLL + inner
            value, image = operate(row, second, ext_two)
            left = resid[row] - image
            done = (first[row] + value) + (keep * value + gain * left)
            total[row] = done
            crossed = jnp.concatenate([done[half + half // 2 :], done[half : half + half // 2]], axis=0)
            term = omega * done[:half] * crossed
            terms[freq, pl.ds(row, 1), :] = jnp.sum(term, axis=0, keepdims=True)
        return carry

    lax.fori_loop(0, blocks // UNROLL, two, 0)

    copies = []
    for step in range(1, peers):
        copy = pltpu.make_async_remote_copy(
            src_ref=terms.at[freq],
            dst_ref=terms.at[freq],
            send_sem=term_send_sem.at[step],
            recv_sem=term_recv_sem.at[step],
            device_id=others[step - 1],
            device_id_type=MESH,
        )
        copy.start()
        copies.append(copy)
    for system, ref in enumerate((fwd_ref, adj_ref)):
        for f in range(count):
            for c in range(4):
                ref[f, c] = total[:, row_of(count, system, f, c), :]
    stores = []
    for at, (source, target) in enumerate(((fwd_ref, fwd_out), (adj_ref, adj_out))):
        stores.append(pltpu.make_async_copy(source, target, load_sem.at[6 + at]))
        stores[-1].start()
    for copy in copies:
        copy.wait()
    whole = terms[0]
    for peer in range(1, peers):
        whole = whole + terms[peer]
    mass_ref[...] = whole
    stores.append(pltpu.make_async_copy(mass_ref, edge_out, load_sem.at[8]))
    stores[-1].start()
    for copy in stores:
        copy.wait()


def finish(
    scale,
    fwd_hbm,
    adj_hbm,
    edge_hbm,
    cells_hbm,
    cond_hbm,
    fwd_out,
    adj_out,
    model_out,
    edge_ref,
    cells_ref,
    cond_ref,
    copy_sem,
):
    pairs = (
        (edge_hbm, edge_ref),
        (cells_hbm, cells_ref),
        (cond_hbm, cond_ref),
        (fwd_hbm, fwd_out),
        (adj_hbm, adj_out),
    )
    copies = []
    for at, (source, target) in enumerate(pairs):
        copies.append(pltpu.make_async_copy(source, target, copy_sem.at[at]))
        copies[-1].start()
    for copy in copies[:3]:
        copy.wait()

    blocks, size = edge_ref.shape
    corners, cells = cells_ref.shape
    shift = size.bit_length() - 1
    sums = []
    for column in range(cells // size):
        acc = jnp.zeros((1, size), jnp.float32)
        for start in range(0, corners, 8):
            rows = min(8, corners - start)
            ids = cells_ref[pl.ds(start, rows), pl.ds(column * size, size)]
            if rows < 8:
                ids = jnp.concatenate([ids, jnp.full((8 - rows, size), -1, jnp.int32)], axis=0)
            block = ids >> shift
            lane = ids & (size - 1)
            found = jnp.zeros((8, size), jnp.float32)
            for row in range(blocks):
                values = jnp.broadcast_to(edge_ref[pl.ds(row, 1), :], (8, size))
                got = jnp.take_along_axis(values, lane, axis=1, mode="promise_in_bounds")
                found = jnp.where(block == row, got, found)
            acc = acc + jnp.sum(found, axis=0, keepdims=True)
        sums.append(acc)
    grad = jnp.concatenate(sums, axis=0) * scale
    model_out[...] = cond_ref[...] - 0.5 * grad / jnp.sqrt(grad * grad + 1.0)
    for copy in copies[3:]:
        copy.wait()


def local(
    fwd_source,
    adj_source,
    curl_blocks,
    block_links,
    tile_lists,
    edge_mass,
    omega,
    cell_edges,
    log_cond,
):
    count, _, blocks, size = fwd_source.shape
    peers = lax.axis_size("freq")
    width = 8 * count
    rounds, tiles = tile_lists.shape
    sent = rounds * tiles
    links = block_links.shape[1]
    cells = log_cond.shape[0]
    cond = log_cond.reshape(cells // size, size)
    f32, bf16 = jnp.float32, jnp.bfloat16
    vmem = pl.BlockSpec(memory_space=pltpu.VMEM)
    hbm = pl.BlockSpec(memory_space=pltpu.HBM)
    fields, adjoint, edge = pl.pallas_call(
        functools.partial(kernel, peers),
        out_shape=(
            jax.ShapeDtypeStruct(fwd_source.shape, f32),
            jax.ShapeDtypeStruct(adj_source.shape, f32),
            jax.ShapeDtypeStruct((blocks, size), f32),
        ),
        in_specs=[hbm] * 7,
        out_specs=(hbm,) * 3,
        scratch_shapes=[
            pltpu.SMEM((links, blocks), jnp.int32),
            pltpu.SMEM((rounds, tiles), jnp.int32),
            pltpu.SMEM((count,), f32),
            pltpu.VMEM(fwd_source.shape, f32),
            pltpu.VMEM(adj_source.shape, f32),
            pltpu.VMEM((blocks, size), f32),
            pltpu.VMEM(curl_blocks.shape, f32),
            pltpu.VMEM((blocks, 2 * size, links * size), bf16),
            pltpu.VMEM((blocks, width // 2, size), f32),
            pltpu.VMEM((blocks, width, size), f32),
            pltpu.VMEM((blocks, width, size), f32),
            pltpu.VMEM((blocks, width, size), f32),
            pltpu.VMEM((blocks, width, size), f32),
            pltpu.VMEM((blocks + sent, width, size), f32),
            pltpu.VMEM((blocks + sent, width, size), f32),
            pltpu.VMEM((sent, width, size), f32),
            pltpu.VMEM((sent, width, size), f32),
            pltpu.VMEM((peers, blocks, size), f32),
            pltpu.SemaphoreType.DMA((9,)),
            pltpu.SemaphoreType.DMA((blocks // CHUNK,)),
            pltpu.SemaphoreType.DMA((2, rounds, 2)),
            pltpu.SemaphoreType.DMA((2, rounds, 2)),
            pltpu.SemaphoreType.DMA((peers,)),
            pltpu.SemaphoreType.DMA((peers,)),
        ],
        compiler_params=pltpu.CompilerParams(
            collective_id=0, has_side_effects=True, vmem_limit_bytes=VMEM
        ),
    )(
        block_links.T,
        tile_lists,
        omega,
        fwd_source,
        adj_source,
        curl_blocks,
        edge_mass,
    )
    scale = 1.0 / (24.0 * count * peers) ** 0.5
    fwd_field, adj_field, model = pl.pallas_call(
        functools.partial(finish, scale),
        out_shape=(
            jax.ShapeDtypeStruct(fwd_source.shape, f32),
            jax.ShapeDtypeStruct(adj_source.shape, f32),
            jax.ShapeDtypeStruct(cond.shape, f32),
        ),
        in_specs=[hbm] * 5,
        out_specs=(hbm, hbm, vmem),
        scratch_shapes=[
            pltpu.VMEM((blocks, size), f32),
            pltpu.VMEM(cell_edges.shape, jnp.int32),
            pltpu.VMEM(cond.shape, f32),
            pltpu.SemaphoreType.DMA((5,)),
        ],
        compiler_params=pltpu.CompilerParams(vmem_limit_bytes=VMEM),
    )(fields, adjoint, edge, cell_edges, cond)
    return fwd_field, adj_field, model.reshape(cells)


def solution(mesh):
    in_specs = (
        P("freq", None, "dom", None),
        P("freq", None, "dom", None),
        P("dom", None, None, None),
        P("dom", None),
        P("dom", None),
        P("dom", None),
        P("freq"),
        P(None, "dom"),
        P("dom"),
    )
    out_specs = (P("freq", None, "dom", None), P("freq", None, "dom", None), P("dom"))
    return jax.shard_map(local, mesh=mesh, in_specs=in_specs, out_specs=out_specs, check_vma=False)
```

time: 39.3 us -> 41.8 us (1.064)
  Pallas kernels: 32.5 us -> 41 us
  local copies, waits for them, and re-layouts: 5.9 us -> 0 us
    pallas_call x1, Pallas kernels: 2.37 us -> 9.68 us  [local(): pl.pallas_call(functools.partial(finish, scale), out_shape=(jax.ShapeDtyp...]
    unnamed x15 -> x0, local copies, waits for them, and re-layouts: 5.9 us -> none
    pallas_call x1, Pallas kernels: 30.1 us -> 31.3 us  [local(): pl.pallas_call(functools.partial(kernel, peers), out_shape=(jax.ShapeDtyp...]
where the time goes in v2:
time: 41.8 us; the launch traced here: 41.6 us
  Pallas kernels  41 us (98%)
  between operations  0.64 us (2%)
    pallas_call x1, Pallas kernels, local(): pl.pallas_call(functools.partial(kernel, peers), out_shape=(jax.ShapeDtyp...  31.3 us
    pallas_call x1, Pallas kernels, local(): pl.pallas_call(functools.partial(finish, scale), out_shape=(jax.ShapeDtyp...  9.68 us

profile of v2, /device:TPU:0, one launch (start us, length us, event | category | flops | bytes accessed | tf_op | source)
XLA Modules:
  0.0 41.6 jit_solution(17698037252795958562)
XLA Ops:
  0.6 31.3 %shard_map.112 = (f32[2,4,32,128]{3,2,1,0:T(8,128)}, f32[2,4,32,128]{3,2,1,0:T(8,128)}, f32[32,128]{1,0:T(8,128)}) custom-call(s32[4,32]{1,0:T(4,128)} %bitcast.4, s32[4,16]{1,0:T(4,128)} %tiles_hbm.1, f32[2]{0:T(128)} %omega_hbm.1, f32[2,4,32,128]{3,2,1,0:T(8,128)} %fwd_hbm.1, f32[2,4,32,128]{3,2,1,0:T(8,128)} %adj_hbm.1, f32[32,4,128,128]{3,2,1,0:T(8,128)} %curl_hbm.1, ...), custom_call_target="tpu_custom_call" | custom-call | tf_op jit(solution)/shard_map/pallas_call | solution.py:353
  31.9 9.7 %shard_map.113 = (f32[2,4,32,128]{3,2,1,0:T(8,128)}, f32[2,4,32,128]{3,2,1,0:T(8,128)}, f32[8,128]{1,0:T(8,128)}) custom-call(f32[2,4,32,128]{3,2,1,0:T(8,128)} %get-tuple-element.9.fwd_hbm, f32[2,4,32,128]{3,2,1,0:T(8,128)} %get-tuple-element.10.adj_hbm, f32[32,128]{1,0:T(8,128)} %get-tuple-element.11.edge_hbm, s32[12,1024]{1,0:T(8,128)} %cells_hbm.1, ...), custom_call_target="tpu_custom_call" | custom-call | tf_op jit(solution)/shard_map/pallas_call | solution.py:401

commit v3 on v2

--- a/solution.py
+++ b/solution.py
@@ -162,10 +162,10 @@
         def cut(step, carry):
             row = chunk * CHUNK + step
             for link in range(links):
-                high, low = split(raw[row, link])
-                columns = pl.ds(link * size, size)
-                parts[row, pl.ds(0, size), columns] = high
-                parts[row, pl.ds(size, size), columns] = low
+                high, low = split(raw[row, link].T)
+                rows = pl.ds(link * size, size)
+                parts[row, rows, pl.ds(0, size)] = high
+                parts[row, rows, pl.ds(size, size)] = low
             return carry
 
         lax.fori_loop(0, CHUNK, cut, 0)
@@ -174,9 +174,7 @@
         gathered = [ext[links_ref[link, row]] for link in range(links)]
         high, low = split(jnp.concatenate(gathered, axis=1))
         both = jnp.concatenate([high, low], axis=0)
-        product = lax.dot_general(
-            both, parts[row], (((1,), (1,)), ((), ())), preferred_element_type=jnp.float32
-        )
+        product = jnp.dot(both, parts[row], preferred_element_type=jnp.float32)
         product = product[:width] + product[width:]
         curl = product[:, :size] + product[:, size:]
         value = field[row]
@@ -286,21 +284,26 @@
     edge_ref,
     cells_ref,
     cond_ref,
+    fwd_ref,
+    adj_ref,
     copy_sem,
 ):
     pairs = (
         (edge_hbm, edge_ref),
         (cells_hbm, cells_ref),
         (cond_hbm, cond_ref),
-        (fwd_hbm, fwd_out),
-        (adj_hbm, adj_out),
+        (fwd_hbm, fwd_ref),
+        (adj_hbm, adj_ref),
+        (fwd_ref, fwd_out),
+        (adj_ref, adj_out),
     )
-    copies = []
-    for at, (source, target) in enumerate(pairs):
-        copies.append(pltpu.make_async_copy(source, target, copy_sem.at[at]))
-        copies[-1].start()
-    for copy in copies[:3]:
-        copy.wait()
+    copies = [pltpu.make_async_copy(*pair, copy_sem.at[at]) for at, pair in enumerate(pairs)]
+    for copy in copies[:5]:
+        copy.start()
+    for copy in copies[:5]:
+        copy.wait()
+    for copy in copies[5:]:
+        copy.start()
 
     blocks, size = edge_ref.shape
     corners, cells = cells_ref.shape
@@ -324,7 +327,7 @@
         sums.append(acc)
     grad = jnp.concatenate(sums, axis=0) * scale
     model_out[...] = cond_ref[...] - 0.5 * grad / jnp.sqrt(grad * grad + 1.0)
-    for copy in copies[3:]:
+    for copy in copies[5:]:
         copy.wait()
 
 
@@ -367,7 +370,7 @@
             pltpu.VMEM(adj_source.shape, f32),
             pltpu.VMEM((blocks, size), f32),
             pltpu.VMEM(curl_blocks.shape, f32),
-            pltpu.VMEM((blocks, 2 * size, links * size), bf16),
+            pltpu.VMEM((blocks, links * size, 2 * size), bf16),
             pltpu.VMEM((blocks, width // 2, size), f32),
             pltpu.VMEM((blocks, width, size), f32),
             pltpu.VMEM((blocks, width, size), f32),
@@ -411,7 +414,9 @@
             pltpu.VMEM((blocks, size), f32),
             pltpu.VMEM(cell_edges.shape, jnp.int32),
             pltpu.VMEM(cond.shape, f32),
-            pltpu.SemaphoreType.DMA((5,)),
+            pltpu.VMEM(fwd_source.shape, f32),
+            pltpu.VMEM(adj_source.shape, f32),
+            pltpu.SemaphoreType.DMA((7,)),
         ],
         compiler_params=pltpu.CompilerParams(vmem_limit_bytes=VMEM),
     )(fields, adjoint, edge, cell_edges, cond)

time: 41.8 us -> 31.5 us (0.75)
  Pallas kernels: 41 us -> 30.6 us
    pallas_call x1, Pallas kernels: 9.68 us -> 2.39 us  [local(): pl.pallas_call(functools.partial(finish, scale), out_shape=(jax.ShapeDtyp...]
    pallas_call x1, Pallas kernels: 31.3 us -> 28.2 us  [local(): pl.pallas_call(functools.partial(kernel, peers), out_shape=(jax.ShapeDtyp...]
where the time goes in v3:
time: 31.5 us; the launch traced here: 31.2 us
  Pallas kernels  30.6 us (97%)
  between operations  0.64 us (2%)
    pallas_call x1, Pallas kernels, local(): pl.pallas_call(functools.partial(kernel, peers), out_shape=(jax.ShapeDtyp...  28.2 us
    pallas_call x1, Pallas kernels, local(): pl.pallas_call(functools.partial(finish, scale), out_shape=(jax.ShapeDtyp...  2.39 us

profile of v3, /device:TPU:0, one launch (start us, length us, event | category | flops | bytes accessed | tf_op | source)
XLA Modules:
  0.0 31.2 jit_solution(216391151090705019)
XLA Ops:
  0.6 28.2 %shard_map.112 = (f32[2,4,32,128]{3,2,1,0:T(8,128)}, f32[2,4,32,128]{3,2,1,0:T(8,128)}, f32[32,128]{1,0:T(8,128)}) custom-call(s32[4,32]{1,0:T(4,128)} %bitcast.4, s32[4,16]{1,0:T(4,128)} %tiles_hbm.1, f32[2]{0:T(128)} %omega_hbm.1, f32[2,4,32,128]{3,2,1,0:T(8,128)} %fwd_hbm.1, f32[2,4,32,128]{3,2,1,0:T(8,128)} %adj_hbm.1, f32[32,4,128,128]{3,2,1,0:T(8,128)} %curl_hbm.1, ...), custom_call_target="tpu_custom_call" | custom-call | tf_op jit(solution)/shard_map/pallas_call | solution.py:356
  28.8 2.4 %shard_map.113 = (f32[2,4,32,128]{3,2,1,0:T(8,128)}, f32[2,4,32,128]{3,2,1,0:T(8,128)}, f32[8,128]{1,0:T(8,128)}) custom-call(f32[2,4,32,128]{3,2,1,0:T(8,128)} %get-tuple-element.9.fwd_hbm, f32[2,4,32,128]{3,2,1,0:T(8,128)} %get-tuple-element.10.adj_hbm, f32[32,128]{1,0:T(8,128)} %get-tuple-element.11.edge_hbm, s32[12,1024]{1,0:T(8,128)} %cells_hbm.1, ...), custom_call_target="tpu_custom_call" | custom-call | tf_op jit(solution)/shard_map/pallas_call | solution.py:404

commit v4 on v3

--- a/solution.py
+++ b/solution.py
@@ -12,7 +12,7 @@
 MESH = pl.DeviceIdType.MESH
 VMEM = 63 * 1024 * 1024
 CHUNK = 4
-UNROLL = 4
+UNROLL = 8
 
 
 def chebyshev_factors():
@@ -194,7 +194,7 @@
         copy.wait()
 
     copies = []
-    for bit in reversed(range(rounds)[-2:]):
+    for bit in reversed(range(rounds)[-1:]):
         for piece in range(pieces):
 
             def ahead(step, carry):
@@ -215,7 +215,7 @@
         return carry
 
     lax.fori_loop(0, blocks // UNROLL, one, 0)
-    for bit in reversed(range(rounds)[:-2]):
+    for bit in reversed(range(rounds)[:-1]):
         for piece in range(pieces):
             for tile in range(piece * span, (piece + 1) * span):
                 send_two[bit * tiles + tile] = second[tiles_ref[bit, tile]]

time: 31.5 us -> 29.7 us (0.943)
  Pallas kernels: 30.6 us -> 28.8 us
    pallas_call x1, Pallas kernels: 28.2 us -> 26.4 us  [local(): pl.pallas_call(functools.partial(kernel, peers), out_shape=(jax.ShapeDtyp...]
where the time goes in v4:
time: 29.7 us; the launch traced here: 29.4 us
  Pallas kernels  28.8 us (97%)
  between operations  0.64 us (2%)
    pallas_call x1, Pallas kernels, local(): pl.pallas_call(functools.partial(kernel, peers), out_shape=(jax.ShapeDtyp...  26.4 us
    pallas_call x1, Pallas kernels, local(): pl.pallas_call(functools.partial(finish, scale), out_shape=(jax.ShapeDtyp...  2.39 us

profile of v4, /device:TPU:0, one launch (start us, length us, event | category | flops | bytes accessed | tf_op | source)
XLA Modules:
  0.0 29.4 jit_solution(9471894217256200675)
XLA Ops:
  0.6 26.4 %shard_map.112 = (f32[2,4,32,128]{3,2,1,0:T(8,128)}, f32[2,4,32,128]{3,2,1,0:T(8,128)}, f32[32,128]{1,0:T(8,128)}) custom-call(s32[4,32]{1,0:T(4,128)} %bitcast.4, s32[4,16]{1,0:T(4,128)} %tiles_hbm.1, f32[2]{0:T(128)} %omega_hbm.1, f32[2,4,32,128]{3,2,1,0:T(8,128)} %fwd_hbm.1, f32[2,4,32,128]{3,2,1,0:T(8,128)} %adj_hbm.1, f32[32,4,128,128]{3,2,1,0:T(8,128)} %curl_hbm.1, ...), custom_call_target="tpu_custom_call" | custom-call | tf_op jit(solution)/shard_map/pallas_call | solution.py:356
  27.0 2.4 %shard_map.113 = (f32[2,4,32,128]{3,2,1,0:T(8,128)}, f32[2,4,32,128]{3,2,1,0:T(8,128)}, f32[8,128]{1,0:T(8,128)}) custom-call(f32[2,4,32,128]{3,2,1,0:T(8,128)} %get-tuple-element.9.fwd_hbm, f32[2,4,32,128]{3,2,1,0:T(8,128)} %get-tuple-element.10.adj_hbm, f32[32,128]{1,0:T(8,128)} %get-tuple-element.11.edge_hbm, s32[12,1024]{1,0:T(8,128)} %cells_hbm.1, ...), custom_call_target="tpu_custom_call" | custom-call | tf_op jit(solution)/shard_map/pallas_call | solution.py:404

commit v5 on v4

--- a/solution.py
+++ b/solution.py
@@ -162,10 +162,10 @@
         def cut(step, carry):
             row = chunk * CHUNK + step
             for link in range(links):
-                high, low = split(raw[row, link].T)
-                rows = pl.ds(link * size, size)
-                parts[row, rows, pl.ds(0, size)] = high
-                parts[row, rows, pl.ds(size, size)] = low
+                high, low = split(raw[row, link])
+                columns = pl.ds(link * size, size)
+                parts[row, pl.ds(0, size), columns] = high
+                parts[row, pl.ds(size, size), columns] = low
             return carry
 
         lax.fori_loop(0, CHUNK, cut, 0)
@@ -174,9 +174,11 @@
         gathered = [ext[links_ref[link, row]] for link in range(links)]
         high, low = split(jnp.concatenate(gathered, axis=1))
         both = jnp.concatenate([high, low], axis=0)
-        product = jnp.dot(both, parts[row], preferred_element_type=jnp.float32)
-        product = product[:width] + product[width:]
-        curl = product[:, :size] + product[:, size:]
+        product = lax.dot_general(
+            parts[row], both, (((1,), (1,)), ((), ())), preferred_element_type=jnp.float32
+        )
+        product = (product[:size] + product[size:]).T
+        curl = product[:width] + product[width:]
         value = field[row]
         turned = jnp.concatenate([-value[half:], value[:half]], axis=0)
         scale = weight[row]
@@ -370,7 +372,7 @@
             pltpu.VMEM(adj_source.shape, f32),
             pltpu.VMEM((blocks, size), f32),
             pltpu.VMEM(curl_blocks.shape, f32),
-            pltpu.VMEM((blocks, links * size, 2 * size), bf16),
+            pltpu.VMEM((blocks, 2 * size, links * size), bf16),
             pltpu.VMEM((blocks, width // 2, size), f32),
             pltpu.VMEM((blocks, width, size), f32),
             pltpu.VMEM((blocks, width, size), f32),

time: 29.7 us -> 32.1 us (1.081)
  Pallas kernels: 28.8 us -> 31.2 us
    pallas_call x1, Pallas kernels: 26.4 us -> 28.8 us  [local(): pl.pallas_call(functools.partial(kernel, peers), out_shape=(jax.ShapeDtyp...]
where the time goes in v5:
time: 32.1 us; the launch traced here: 31.9 us
  Pallas kernels  31.2 us (97%)
  between operations  0.64 us (2%)
    pallas_call x1, Pallas kernels, local(): pl.pallas_call(functools.partial(kernel, peers), out_shape=(jax.ShapeDtyp...  28.8 us
    pallas_call x1, Pallas kernels, local(): pl.pallas_call(functools.partial(finish, scale), out_shape=(jax.ShapeDtyp...  2.39 us

profile of v5, /device:TPU:0, one launch (start us, length us, event | category | flops | bytes accessed | tf_op | source)
XLA Modules:
  0.0 31.9 jit_solution(13529251655433593654)
XLA Ops:
  0.6 28.8 %shard_map.112 = (f32[2,4,32,128]{3,2,1,0:T(8,128)}, f32[2,4,32,128]{3,2,1,0:T(8,128)}, f32[32,128]{1,0:T(8,128)}) custom-call(s32[4,32]{1,0:T(4,128)} %bitcast.4, s32[4,16]{1,0:T(4,128)} %tiles_hbm.1, f32[2]{0:T(128)} %omega_hbm.1, f32[2,4,32,128]{3,2,1,0:T(8,128)} %fwd_hbm.1, f32[2,4,32,128]{3,2,1,0:T(8,128)} %adj_hbm.1, f32[32,4,128,128]{3,2,1,0:T(8,128)} %curl_hbm.1, ...), custom_call_target="tpu_custom_call" | custom-call | tf_op jit(solution)/shard_map/pallas_call | solution.py:358
  29.5 2.4 %shard_map.113 = (f32[2,4,32,128]{3,2,1,0:T(8,128)}, f32[2,4,32,128]{3,2,1,0:T(8,128)}, f32[8,128]{1,0:T(8,128)}) custom-call(f32[2,4,32,128]{3,2,1,0:T(8,128)} %get-tuple-element.9.fwd_hbm, f32[2,4,32,128]{3,2,1,0:T(8,128)} %get-tuple-element.10.adj_hbm, f32[32,128]{1,0:T(8,128)} %get-tuple-element.11.edge_hbm, s32[12,1024]{1,0:T(8,128)} %cells_hbm.1, ...), custom_call_target="tpu_custom_call" | custom-call | tf_op jit(solution)/shard_map/pallas_call | solution.py:406

commit v6 on v4

--- a/solution.py
+++ b/solution.py
@@ -55,7 +55,9 @@
     adj_ref,
     mass_ref,
     raw,
+    parts_own,
     parts,
+    near,
     weight,
     first,
     second,
@@ -163,33 +165,88 @@
             row = chunk * CHUNK + step
             for link in range(links):
                 high, low = split(raw[row, link].T)
-                rows = pl.ds(link * size, size)
-                parts[row, rows, pl.ds(0, size)] = high
-                parts[row, rows, pl.ds(size, size)] = low
+                if link == 0:
+                    parts_own[row, :, pl.ds(0, size)] = high
+                    parts_own[row, :, pl.ds(size, size)] = low
+                else:
+                    rows = pl.ds((link - 1) * size, size)
+                    parts[row, rows, pl.ds(0, size)] = high
+                    parts[row, rows, pl.ds(size, size)] = low
             return carry
 
         lax.fori_loop(0, CHUNK, cut, 0)
 
-    def operate(row, field, ext):
-        gathered = [ext[links_ref[link, row]] for link in range(links)]
-        high, low = split(jnp.concatenate(gathered, axis=1))
-        both = jnp.concatenate([high, low], axis=0)
-        product = jnp.dot(both, parts[row], preferred_element_type=jnp.float32)
+    def stacked(value):
+        return jnp.concatenate(split(value), axis=0)
+
+    def folded(product):
         product = product[:width] + product[width:]
-        curl = product[:, :size] + product[:, size:]
+        return product[:, :size] + product[:, size:]
+
+    def times(left, right):
+        return jnp.dot(left, right, preferred_element_type=jnp.float32)
+
+    def paired(one_left, two_left, one_right, two_right):
+        blank = jnp.zeros_like(one_left)
+        upper = jnp.concatenate([one_left, blank], axis=1)
+        lower = jnp.concatenate([blank, two_left], axis=1)
+        product = times(
+            jnp.concatenate([upper, lower], axis=0),
+            jnp.concatenate([one_right, two_right], axis=0),
+        )
+        return folded(product[: 2 * width]), folded(product[2 * width :])
+
+    def own_blocks(field):
+        def body(step, carry):
+            for inner in range(0, UNROLL, 2):
+                row = step * UNROLL + inner
+                near[row], near[row + 1] = paired(
+                    stacked(field[row]),
+                    stacked(field[row + 1]),
+                    parts_own[row],
+                    parts_own[row + 1],
+                )
+            return carry
+
+        lax.fori_loop(0, blocks // UNROLL, body, 0)
+
+    def close(row, field, curl):
         value = field[row]
         turned = jnp.concatenate([-value[half:], value[:half]], axis=0)
         scale = weight[row]
-        return value, curl + jnp.concatenate([scale, scale], axis=0) * turned
+        return value, curl + near[row] + jnp.concatenate([scale, scale], axis=0) * turned
+
+    def operate(row, field, ext):
+        gathered = [ext[links_ref[link, row]] for link in range(1, links)]
+        left = stacked(jnp.concatenate(gathered, axis=1))
+        return close(row, field, folded(times(left, parts[row])))
+
+    def operate_two(row, field, ext):
+        depth = (links - 2) * size
+        curls = []
+        for at in (row, row + 1):
+            gathered = [ext[links_ref[link, at]] for link in range(1, links - 1)]
+            left = stacked(jnp.concatenate(gathered, axis=1))
+            curls.append(folded(times(left, parts[at, pl.ds(0, depth)])))
+        last = paired(
+            stacked(ext[links_ref[links - 1, row]]),
+            stacked(ext[links_ref[links - 1, row + 1]]),
+            parts[row, pl.ds(depth, size)],
+            parts[row + 1, pl.ds(depth, size)],
+        )
+        return [
+            close(at, field, curl + extra)
+            for at, curl, extra in zip((row, row + 1), curls, last)
+        ]
 
     factors = chebyshev_factors()
 
-    def advance(row):
+    def advance(value, image):
         keep, gain = factors[0]
-        value, image = operate(row, first, ext_one)
         left = value - image
         return left, keep * value + gain * left
 
+    own_blocks(first)
     for copy in copies:
         copy.wait()
 
@@ -200,18 +257,20 @@
             def ahead(step, carry):
                 for inner in range(UNROLL):
                     tile = piece * span + step * UNROLL + inner
-                    send_two[bit * tiles + tile] = advance(tiles_ref[bit, tile])[1]
+                    done = advance(*operate(tiles_ref[bit, tile], first, ext_one))
+                    send_two[bit * tiles + tile] = done[1]
                 return carry
 
             lax.fori_loop(0, span // UNROLL, ahead, 0)
             copies.append(push(send_two, ext_two, 1, bit, piece))
 
     def one(step, carry):
-        for inner in range(UNROLL):
+        for inner in range(0, UNROLL, 2):
             row = step * UNROLL + inner
-            left, value = advance(row)
-            resid[row] = left
-            second[row] = value
+            for at, pair in enumerate(operate_two(row, first, ext_one)):
+                left, value = advance(*pair)
+                resid[row + at] = left
+                second[row + at] = value
         return carry
 
     lax.fori_loop(0, blocks // UNROLL, one, 0)
@@ -221,20 +280,24 @@
                 send_two[bit * tiles + tile] = second[tiles_ref[bit, tile]]
             copies.append(push(send_two, ext_two, 1, bit, piece))
     ext_two[pl.ds(0, blocks)] = second[...]
+    own_blocks(second)
     for copy in copies:
         copy.wait()
 
     def two(step, carry):
         keep, gain = factors[1]
-        for inner in range(UNROLL):
-            row = step * UNROLL + inner
-            value, image = operate(row, second, ext_two)
-            left = resid[row] - image
-            done = (first[row] + value) + (keep * value + gain * left)
-            total[row] = done
-            crossed = jnp.concatenate([done[half + half // 2 :], done[half : half + half // 2]], axis=0)
-            term = omega * done[:half] * crossed
-            terms[freq, pl.ds(row, 1), :] = jnp.sum(term, axis=0, keepdims=True)
+        for inner in range(0, UNROLL, 2):
+            start = step * UNROLL + inner
+            for at, (value, image) in enumerate(operate_two(start, second, ext_two)):
+                row = start + at
+                left = resid[row] - image
+                done = (first[row] + value) + (keep * value + gain * left)
+                total[row] = done
+                crossed = jnp.concatenate(
+                    [done[half + half // 2 :], done[half : half + half // 2]], axis=0
+                )
+                term = omega * done[:half] * crossed
+                terms[freq, pl.ds(row, 1), :] = jnp.sum(term, axis=0, keepdims=True)
         return carry
 
     lax.fori_loop(0, blocks // UNROLL, two, 0)
@@ -370,7 +433,9 @@
             pltpu.VMEM(adj_source.shape, f32),
             pltpu.VMEM((blocks, size), f32),
             pltpu.VMEM(curl_blocks.shape, f32),
-            pltpu.VMEM((blocks, links * size, 2 * size), bf16),
+            pltpu.VMEM((blocks, size, 2 * size), bf16),
+            pltpu.VMEM((blocks, (links - 1) * size, 2 * size), bf16),
+            pltpu.VMEM((blocks, width, size), f32),
             pltpu.VMEM((blocks, width // 2, size), f32),
             pltpu.VMEM((blocks, width, size), f32),
             pltpu.VMEM((blocks, width, size), f32),

time: 29.7 us -> 29.2 us (0.983)
  Pallas kernels: 28.8 us -> 28.4 us
    pallas_call x1, Pallas kernels: 26.4 us -> 26 us  [local(): pl.pallas_call(functools.partial(kernel, peers), out_shape=(jax.ShapeDtyp...]
where the time goes in v6:
time: 29.2 us; the launch traced here: 29 us
  Pallas kernels  28.4 us (97%)
  between operations  0.64 us (2%)
    pallas_call x1, Pallas kernels, local(): pl.pallas_call(functools.partial(kernel, peers), out_shape=(jax.ShapeDtyp...  26 us
    pallas_call x1, Pallas kernels, local(): pl.pallas_call(functools.partial(finish, scale), out_shape=(jax.ShapeDtyp...  2.39 us

profile of v6, /device:TPU:0, one launch (start us, length us, event | category | flops | bytes accessed | tf_op | source)
XLA Modules:
  0.0 29.0 jit_solution(8307650050537088265)
XLA Ops:
  0.6 26.0 %shard_map.112 = (f32[2,4,32,128]{3,2,1,0:T(8,128)}, f32[2,4,32,128]{3,2,1,0:T(8,128)}, f32[32,128]{1,0:T(8,128)}) custom-call(s32[4,32]{1,0:T(4,128)} %bitcast.4, s32[4,16]{1,0:T(4,128)} %tiles_hbm.1, f32[2]{0:T(128)} %omega_hbm.1, f32[2,4,32,128]{3,2,1,0:T(8,128)} %fwd_hbm.1, f32[2,4,32,128]{3,2,1,0:T(8,128)} %adj_hbm.1, f32[32,4,128,128]{3,2,1,0:T(8,128)} %curl_hbm.1, ...), custom_call_target="tpu_custom_call" | custom-call | tf_op jit(solution)/shard_map/pallas_call | solution.py:419
  26.6 2.4 %shard_map.113 = (f32[2,4,32,128]{3,2,1,0:T(8,128)}, f32[2,4,32,128]{3,2,1,0:T(8,128)}, f32[8,128]{1,0:T(8,128)}) custom-call(f32[2,4,32,128]{3,2,1,0:T(8,128)} %get-tuple-element.9.fwd_hbm, f32[2,4,32,128]{3,2,1,0:T(8,128)} %get-tuple-element.10.adj_hbm, f32[32,128]{1,0:T(8,128)} %get-tuple-element.11.edge_hbm, s32[12,1024]{1,0:T(8,128)} %cells_hbm.1, ...), custom_call_target="tpu_custom_call" | custom-call | tf_op jit(solution)/shard_map/pallas_call | solution.py:469

commit v7 on v6

--- a/solution.py
+++ b/solution.py
@@ -12,7 +12,7 @@
 MESH = pl.DeviceIdType.MESH
 VMEM = 63 * 1024 * 1024
 CHUNK = 4
-UNROLL = 8
+UNROLL = 16
 
 
 def chebyshev_factors():
@@ -123,6 +123,7 @@
 
     pieces = 2
     span = tiles // pieces
+    group = min(UNROLL, span)
 
     def push(send, ext, phase, bit, piece):
         rows = bit * tiles + piece * span
@@ -255,13 +256,13 @@
         for piece in range(pieces):
 
             def ahead(step, carry):
-                for inner in range(UNROLL):
-                    tile = piece * span + step * UNROLL + inner
+                for inner in range(group):
+                    tile = piece * span + step * group + inner
                     done = advance(*operate(tiles_ref[bit, tile], first, ext_one))
                     send_two[bit * tiles + tile] = done[1]
                 return carry
 
-            lax.fori_loop(0, span // UNROLL, ahead, 0)
+            lax.fori_loop(0, span // group, ahead, 0)
             copies.append(push(send_two, ext_two, 1, bit, piece))
 
     def one(step, carry):

time: 29.2 us -> 28.9 us (0.990)
  Pallas kernels: 28.4 us -> 28 us
    pallas_call x1, Pallas kernels: 26 us -> 25.7 us  [local(): pl.pallas_call(functools.partial(kernel, peers), out_shape=(jax.ShapeDtyp...]
where the time goes in v7:
time: 28.9 us; the launch traced here: 28.7 us
  Pallas kernels  28 us (97%)
  between operations  0.64 us (2%)
    pallas_call x1, Pallas kernels, local(): pl.pallas_call(functools.partial(kernel, peers), out_shape=(jax.ShapeDtyp...  25.7 us
    pallas_call x1, Pallas kernels, local(): pl.pallas_call(functools.partial(finish, scale), out_shape=(jax.ShapeDtyp...  2.39 us

profile of v7, /device:TPU:0, one launch (start us, length us, event | category | flops | bytes accessed | tf_op | source)
XLA Modules:
  0.0 28.7 jit_solution(11800951667978273295)
XLA Ops:
  0.6 25.7 %shard_map.112 = (f32[2,4,32,128]{3,2,1,0:T(8,128)}, f32[2,4,32,128]{3,2,1,0:T(8,128)}, f32[32,128]{1,0:T(8,128)}) custom-call(s32[4,32]{1,0:T(4,128)} %bitcast.4, s32[4,16]{1,0:T(4,128)} %tiles_hbm.1, f32[2]{0:T(128)} %omega_hbm.1, f32[2,4,32,128]{3,2,1,0:T(8,128)} %fwd_hbm.1, f32[2,4,32,128]{3,2,1,0:T(8,128)} %adj_hbm.1, f32[32,4,128,128]{3,2,1,0:T(8,128)} %curl_hbm.1, ...), custom_call_target="tpu_custom_call" | custom-call | tf_op jit(solution)/shard_map/pallas_call | solution.py:420
  26.3 2.4 %shard_map.113 = (f32[2,4,32,128]{3,2,1,0:T(8,128)}, f32[2,4,32,128]{3,2,1,0:T(8,128)}, f32[8,128]{1,0:T(8,128)}) custom-call(f32[2,4,32,128]{3,2,1,0:T(8,128)} %get-tuple-element.9.fwd_hbm, f32[2,4,32,128]{3,2,1,0:T(8,128)} %get-tuple-element.10.adj_hbm, f32[32,128]{1,0:T(8,128)} %get-tuple-element.11.edge_hbm, s32[12,1024]{1,0:T(8,128)} %cells_hbm.1, ...), custom_call_target="tpu_custom_call" | custom-call | tf_op jit(solution)/shard_map/pallas_call | solution.py:470
